TPU v7x, 512 devices: a whole 4x8x8 slice. The times are simulated.
512 devices in a mesh: gx: 32 (over z, y_hi), gy: 4 (over y_lo, core), gz: 4 (over x).
Axes of the slice: x: 4, y: 8 (y_hi: 4, y_lo: 2; y = y_hi * 2 + y_lo), z: 8, core: 2. Of those that a mesh axis runs over, the one named last changes fastest.
Arguments:
- activations: bfloat16 [128, 8192], P(None, ('gx', 'gy', 'gz')), may hold values from -24 to 24
- w_qkv: bfloat16 [8192, 10240], P('gx', ('gy', 'gz')), may hold values from -0.0625 to 0.0625
- k_cache: bfloat16 [128, 4096, 8, 128], P(('gx', 'gz'), None, 'gy'), may hold values from -1000 to 1000
- v_cache: bfloat16 [128, 4096, 8, 128], P(('gx', 'gz'), None, 'gy'), may hold values from -6 to 6
- lengths: int32 [128], P(('gx', 'gz')), may hold values from 256 to 4096, as said below
- w_out: bfloat16 [8192, 8192], P(('gy', 'gz'), 'gx'), may hold values from -0.125 to 0.125
Outputs:
- update: bfloat16 [128, 8192], P(None, ('gx', 'gy', 'gz'))
Inputs may be any that keep to these rules, and one draw needn't show every extreme that they name: `lengths`: some sequence has exactly 4096 cached tokens.
All inputs are finite; a program needn't handle non-finite values.
Results may differ from a plain program's by a relative error of at most 0.0085.
The roundings to bfloat16 on the way count: a program that leaves them out, or rounds other values in their place, can miss the bound.
Values may be sent and summed in bfloat16 or wider, within the bound.
No kernel may reach another device: no remote copies, remote signals or barrier semaphores. Data moves between devices by JAX's collectives and lax.ppermute only.
A program may use at most 64 MiB of HBM per device.

v0:
```python
import math

import jax
import jax.numpy as jnp
from jax import lax
from jax.sharding import PartitionSpec as P

ROPE_BASE = 500000.0


def rotate(values, position):
    half_dim = values.shape[-1] // 2
    freqs = jnp.exp(
        jnp.arange(half_dim, dtype=jnp.float32) * (-2.0 * math.log(ROPE_BASE) / values.shape[-1])
    )
    angles = position * freqs
    cosine = jnp.cos(angles)
    sine = jnp.sin(angles)
    first_half = values[..., :half_dim]
    second_half = values[..., half_dim:]
    return jnp.concatenate(
        [first_half * cosine - second_half * sine, second_half * cosine + first_half * sine],
        axis=-1,
    )


def shards(activations, w_qkv, k_cache, v_cache, lengths, w_out):
    out_cols = w_qkv.shape[1]
    groups = k_cache.shape[2]
    head_dim = k_cache.shape[3]
    span = k_cache.shape[1]
    per_half = out_cols // head_dim - 1
    heads_here = 2 * per_half
    partial_terms = jnp.dot(
        lax.all_gather(activations, ("gy", "gz"), axis=1, tiled=True),
        w_qkv,
        preferred_element_type=jnp.float32,
    )
    own_rows = lax.psum_scatter(partial_terms, "gx", scatter_dimension=0, tiled=True).astype(
        jnp.bfloat16
    )
    local_row = lax.all_to_all(own_rows, "gz", split_axis=0, concat_axis=1, tiled=True)
    blocks = local_row.reshape(groups, 2, per_half + 1, head_dim)
    position = lengths[0]
    place = position.astype(jnp.float32)
    queries = rotate(
        blocks[:, :, :per_half].reshape(groups, heads_here, head_dim).astype(jnp.float32), place
    ).astype(jnp.bfloat16)
    key_new = rotate(blocks[:, 0, per_half].astype(jnp.float32), place).astype(jnp.bfloat16)
    value_new = blocks[:, 1, per_half]
    score_scale = 1.0 / math.sqrt(head_dim)
    keys_old = k_cache[0]
    values_old = v_cache[0]
    own_score = (
        jnp.einsum("ghd,gd->gh", queries, key_new, preferred_element_type=jnp.float32) * score_scale
    )
    scores = (
        jnp.einsum("ghd,sgd->ghs", queries, keys_old, preferred_element_type=jnp.float32)
        * score_scale
    )
    spots = lax.broadcasted_iota(jnp.int32, (1, 1, span), 2)
    scores = jnp.where(spots < position, scores, -jnp.inf)
    highest = jnp.maximum(jnp.max(scores, axis=-1), own_score)
    exponent = jnp.exp(scores - highest[..., None])
    own_exponent = jnp.exp(own_score - highest)
    denominator = jnp.sum(exponent, axis=-1) + own_exponent
    weights = (exponent / denominator[..., None]).astype(jnp.bfloat16)
    own_weight = (own_exponent / denominator).astype(jnp.bfloat16)
    new_term = own_weight.astype(jnp.float32)[..., None] * value_new.astype(jnp.float32)[:, None, :]
    attended = new_term + jnp.einsum(
        "ghs,sgd->ghd", weights, values_old, preferred_element_type=jnp.float32
    )
    attended_row = attended.astype(jnp.bfloat16).reshape(1, groups * heads_here * head_dim)
    head_rows = w_out.shape[0]
    head_offset = lax.axis_index("gz") * head_rows
    mine = lax.dynamic_slice_in_dim(
        lax.all_gather(attended_row, ("gx", "gz"), axis=0, tiled=True), head_offset, head_rows, 1
    )
    out_terms = jnp.dot(mine, w_out, preferred_element_type=jnp.float32)
    return lax.psum_scatter(out_terms, ("gy", "gz"), scatter_dimension=1, tiled=True).astype(
        jnp.bfloat16
    )


def solution(mesh):
    placed = (
        P(None, ("gx", "gy", "gz")),
        P("gx", ("gy", "gz")),
        P(("gx", "gz"), None, "gy", None),
        P(("gx", "gz"), None, "gy", None),
        P(("gx", "gz")),
        P(("gy", "gz"), "gx"),
    )
    return jax.shard_map(
        shards, mesh=mesh, in_specs=placed, out_specs=P(None, ("gx", "gy", "gz")), check_vma=False
    )
```

profile of v0, /device:TPU:1, one launch (start us, length us, event | category | flops | bytes accessed | tf_op | source)
XLA Modules:
  0.0 656.7 jit_solution(10987419396802337853)
XLA Ops:
  6.5 0.0 copy-start
  6.5 31.1 %all_gather.6 = bf16[128,256]{0,1:T(8,128)(2,1)S(1)} all-gather(bf16[128,16]{0,1:T(8,128)(2,1)} %param.6), channel_id=1, replica_groups=mesh['gx'=32,'gy'=4,'gz'=4] {'gy','gz'}, dimensions={1}, use_global_device_ids=true | all-gather | bytes 69632 | tf_op jit(solution)/shard_map/all_gather | solution.py:35
  37.7 1.2 fusion.24
  38.9 137.2 %all-reduce.2 = bf16[128,640]{1,0:T(8,128)(2,1)S(1)} all-reduce(f32[128,640]{1,0:T(8,128)S(1)} %fusion.24), channel_id=2, replica_groups=mesh['gx'=32,'gy'=4,'gz'=4] {'gx'}, use_global_device_ids=true, to_apply=%region_0.0.clone | all-reduce | flops 81920 | bytes 491520
  176.1 1.3 dynamic-slice.1
  178.0 0.5 broadcast.62
  178.6 0.7 reduce.1
  179.2 0.7 reshape.66
  179.9 3.5 all-to-all-start
  183.4 0.0 reduce-scatter.2.cloned.1.call-start
  184.1 0.1 fusion.18
  184.2 3.7 all-to-all-done
  187.9 0.1 reshape.67
  188.0 0.0 copy-start.2
  188.1 0.1 subtract_convert_fusion.1
  188.2 0.1 subtract_convert_fusion
  188.2 0.1 maximum_bitcast_fusion
  188.3 0.2 fusion.15
  188.5 0.0 copy-done
  188.5 0.8 fusion.23
  189.3 0.2 fusion.10
  189.5 0.1 copy-done.2
  189.6 0.0 copy-start.1
  189.6 0.5 fusion.7
  190.1 318.3 %all-gather = bf16[128,1,2048]{2,1,0:T(2,128)(2,1)S(1)} all-gather(bf16[1,1,2048]{2,1,0:T(2,128)(2,1)S(1)} %reshape.58), channel_id=1, replica_groups=mesh['gx'=32,'gy'=4,'gz'=4] {'gx','gz'}, dimensions={0}, use_global_device_ids=true | all-gather | bytes 528384 | tf_op jit(solution)/shard_map/all_gather | solution.py:77
  508.4 0.3 constant_dynamic-slice_fusion
  508.7 0.0 copy-done.1
  508.7 0.9 fusion.11
  509.6 0.0 reduce-scatter.2.cloned.1.call-update
  509.6 139.0 %reduce-scatter.2.cloned.1.call-done = f32[128,16]{0,1:T(8,128)} async-done(((f32[128,256]{0,1:T(8,128)}), f32[128,16]{0,1:T(8,128)}) %reduce-scatter.2.cloned.1.call-update) | async-done | bytes 8208 | tf_op jit(solution)/shard_map/reduce_scatter | solution.py:80
  648.6 1.3 convert_element_type.57
  (10 shorter events, 0.1 us)
Async XLA Ops:
  6.5 182.0 %copy-start = (bf16[1,4096,2,128]{3,2,1,0:T(2,128)(2,1)S(1)}, bf16[1,4096,2,128]{3,2,1,0:T(2,128)(2,1)}, u32[]{:S(2)}) copy-start(bf16[1,4096,2,128]{3,2,1,0:T(2,128)(2,1)} %param.8) | copy-start | bytes 6291460
  179.9 8.0 %all-to-all-start = ((bf16[4,2,320]{2,1,0:T(2,128)(2,1)}), bf16[4,2,320]{2,1,0:T(2,128)(2,1)S(1)}, u32[]{:S(2)}, u32[]{:S(2)}) async-start(bf16[4,2,320]{2,1,0:T(2,128)(2,1)} %reshape.66), calls=%async_computation | async-start | bytes 12288 | tf_op jit(solution)/shard_map/all_to_all | solution.py:42
  183.4 465.1 %reduce-scatter.2.cloned.1.call-start = ((), (), s32[]{:S(2)}) async-start(), calls=%async_computation.2 | async-start | bytes 139264 | tf_op jit(solution)/shard_map/reduce_scatter | solution.py:80
  188.0 1.6 copy-start.2
  189.6 319.0 %copy-start.1 = (bf16[512,256]{1,0:T(8,128)(2,1)S(1)}, bf16[512,256]{1,0:T(8,128)(2,1)}, u32[]{:S(2)}) copy-start(bf16[512,256]{1,0:T(8,128)(2,1)} %param.11) | copy-start | bytes 786436
Sparse Core Ops, SparseCore 0:
  509.7 138.7 reduce-scatter.1
where the time goes:
time: 658 us; the launch traced here: 657 us
  blocking collectives  487 us (74%)
  waiting for transfers between devices  143 us (22%)
  between operations  14.8 us (2%)
    all_gather x1, blocking collectives, shards(): lax.all_gather(attended_row, ('gx', 'gz'), axis=0, tiled=True)  318 us
    reduce_scatter x1, waiting for transfers between devices, shards(): lax.psum_scatter(out_terms, ('gy', 'gz'), scatter_dimension=1, tiled=True)  139 us
    unnamed x1, blocking collectives  137 us
    all_gather x1, blocking collectives, shards(): lax.all_gather(activations, ('gy', 'gz'), axis=1, tiled=True)  31.1 us
  transfers between devices with their start and end apart: 2, of which 2 were waited for; matrix products, arithmetic and copies ran while one was open for 0% of the time, Pallas kernels for 0%

commit v1 on v0

--- a/solution.py
+++ b/solution.py
@@ -24,6 +24,10 @@
     )
 
 
+def exchange(values, axes):
+    return lax.all_to_all(values, axes, split_axis=0, concat_axis=0, tiled=True)
+
+
 def shards(activations, w_qkv, k_cache, v_cache, lengths, w_out):
     out_cols = w_qkv.shape[1]
     groups = k_cache.shape[2]
@@ -31,15 +35,19 @@
     span = k_cache.shape[1]
     per_half = out_cols // head_dim - 1
     heads_here = 2 * per_half
-    partial_terms = jnp.dot(
-        lax.all_gather(activations, ("gy", "gz"), axis=1, tiled=True),
+    mine_t = exchange(jnp.broadcast_to(activations.T, (16,) + activations.T.shape), ("gy", "gz"))
+    partial_terms = jnp.einsum(
+        "ks,kn->sn",
+        mine_t.reshape(-1, mine_t.shape[-1]),
         w_qkv,
         preferred_element_type=jnp.float32,
     )
-    own_rows = lax.psum_scatter(partial_terms, "gx", scatter_dimension=0, tiled=True).astype(
-        jnp.bfloat16
-    )
-    local_row = lax.all_to_all(own_rows, "gz", split_axis=0, concat_axis=1, tiled=True)
+    rows = partial_terms.shape[0]
+    sent = partial_terms.reshape(rows, out_cols // head_dim, 1, head_dim)
+    received = exchange(sent, ("gx", "gz"))
+    local_row = jnp.sum(
+        received.reshape(32, 4, out_cols // head_dim, head_dim), axis=0
+    ).astype(jnp.bfloat16)
     blocks = local_row.reshape(groups, 2, per_half + 1, head_dim)
     position = lengths[0]
     place = position.astype(jnp.float32)
@@ -70,16 +78,20 @@
     attended = new_term + jnp.einsum(
         "ghs,sgd->ghd", weights, values_old, preferred_element_type=jnp.float32
     )
-    attended_row = attended.astype(jnp.bfloat16).reshape(1, groups * heads_here * head_dim)
-    head_rows = w_out.shape[0]
-    head_offset = lax.axis_index("gz") * head_rows
-    mine = lax.dynamic_slice_in_dim(
-        lax.all_gather(attended_row, ("gx", "gz"), axis=0, tiled=True), head_offset, head_rows, 1
+    w_rows = lax.all_gather(w_out, "gz", axis=0, tiled=True)
+    heads = groups * heads_here
+    pieces = attended.astype(jnp.bfloat16).reshape(heads, head_dim)
+    mine = exchange(jnp.broadcast_to(pieces, (32, heads, head_dim)), "gx")
+    ours = lax.broadcasted_iota(jnp.int32, (1, 4, 1, 1), 1) == lax.axis_index("gz")
+    spread = jnp.where(ours, mine[:, None], 0).astype(jnp.bfloat16)
+    out_terms = jnp.einsum(
+        "sk,kn->ns",
+        spread.reshape(rows, heads * head_dim),
+        w_rows,
+        preferred_element_type=jnp.float32,
     )
-    out_terms = jnp.dot(mine, w_out, preferred_element_type=jnp.float32)
-    return lax.psum_scatter(out_terms, ("gy", "gz"), scatter_dimension=1, tiled=True).astype(
-        jnp.bfloat16
-    )
+    out_parts = exchange(out_terms.reshape(16, -1, rows), ("gy", "gz"))
+    return jnp.sum(out_parts, axis=0).astype(jnp.bfloat16).T
 
 
 def solution(mesh):

time: 658 us -> 96 us (0.15)
  blocking collectives: 487 us -> 11.1 us
  waiting for transfers between devices: 143 us -> 32.1 us
  starting transfers between devices: 3.54 us -> 28.9 us
    all_gather x2 -> x0, blocking collectives: 349 us -> none  [the longest x1 318 us: shards(): lax.all_gather(attended_row, ('gx', 'gz'), axis=0, tiled=True)]
    reduce_scatter x1 -> x0, waiting for transfers between devices: 139 us -> none  [shards(): lax.psum_scatter(out_terms, ('gy', 'gz'), scatter_dimension=1, tiled=True)]
    unnamed x1 -> x0, blocking collectives: 137 us -> none
    all_to_all x1 -> x3, waiting for transfers between devices: 3.72 us -> 31.4 us  [exchange(): return lax.all_to_all(values, axes, split_axis=0, concat_axis=0, tiled=True)]
    all_to_all x1 -> x3, starting transfers between devices: 3.54 us -> 28.8 us  [exchange(): return lax.all_to_all(values, axes, split_axis=0, concat_axis=0, tiled=True)]
    all_to_all x0 -> x1, blocking collectives: none -> 11.1 us  [exchange(): return lax.all_to_all(values, axes, split_axis=0, concat_axis=0, tiled=True)]
  transfers between devices with their start and end apart: 2 -> 4, of which waited for: 2 -> 3; matrix products, arithmetic and copies ran while one was open for 0% -> 4% of each run, Pallas kernels for 0% -> 0%
where the time goes in v1:
time: 96 us; the launch traced here: 95.5 us
  waiting for transfers between devices  32.1 us (33%)
  starting transfers between devices  28.9 us (30%)
  between operations  14.2 us (15%)
  blocking collectives  11.1 us (12%)
  local copies, waits for them, and re-layouts  4.82 us (5%)
  matrix products  3.23 us (3%)
  other arithmetic  1.21 us (1%)
    all_to_all x3, waiting for transfers between devices, exchange(): return lax.all_to_all(values, axes, split_axis=0, concat_axis=0, tiled=True)  31.4 us
    all_to_all x3, starting transfers between devices, exchange(): return lax.all_to_all(values, axes, split_axis=0, concat_axis=0, tiled=True)  28.8 us
    all_to_all x1, blocking collectives, exchange(): return lax.all_to_all(values, axes, split_axis=0, concat_axis=0, tiled=True)  11.1 us
  transfers between devices with their start and end apart: 4, of which 3 were waited for; matrix products, arithmetic and copies ran while one was open for 4% of the time, Pallas kernels for 0%

profile of v1, /device:TPU:1, one launch (start us, length us, event | category | flops | bytes accessed | tf_op | source)
XLA Modules:
  0.0 95.5 jit_solution(11156193298061162189)
XLA Ops:
  6.5 0.0 copy-start
  6.5 1.5 %broadcast_in_dim.60 = bf16[16,16,128]{2,1,0:T(8,128)(2,1)} broadcast(bf16[16,128]{1,0:T(8,128)(2,1)} %bitcast.54), dimensions={1,2} | broadcast | bytes 69632 | tf_op jit(solution)/shard_map/broadcast_in_dim | solution.py:38
  8.0 10.2 %all-to-all-start = ((bf16[16,16,128]{2,1,0:T(8,128)(2,1)}), bf16[16,16,128]{2,1,0:T(8,128)(2,1)S(1)}, u32[]{:S(2)}, u32[]{:S(2)}) async-start(bf16[16,16,128]{2,1,0:T(8,128)(2,1)} %broadcast_in_dim.60), calls=%async_computation | async-start | bytes 131072 | tf_op jit(solution)/shard_map/all_to_all | solution.py:28
  18.2 1.1 %copy.34 = bf16[256,640]{0,1:T(8,128)(2,1)S(1)} copy(bf16[256,640]{1,0:T(8,128)(2,1)} %param.7) | data formatting | bytes 655360 | tf_op args[1]
  19.3 4.7 %all-to-all-done = bf16[16,16,128]{2,1,0:T(8,128)(2,1)S(1)} async-done(((bf16[16,16,128]{2,1,0:T(8,128)(2,1)}), bf16[16,16,128]{2,1,0:T(8,128)(2,1)S(1)}, u32[]{:S(2)}, u32[]{:S(2)}) %all-to-all-start) | async-done | bytes 65568 | tf_op jit(solution)/shard_map/all_to_all | solution.py:28
  24.0 0.2 convolution_bitcast_fusion
  24.3 1.1 %copy.36 = f32[128,5,1,128]{3,2,1,0:T(1,128)} copy(f32[128,5,1,128]{3,0,1,2:T(8,128)S(1)} %convolution_bitcast_fusion) | data formatting | bytes 655360 | tf_op jit(solution)/shard_map/ks,kn->sn/dot_general | solution.py:39
  25.4 14.1 %all-to-all-start.1 = ((f32[128,5,1,128]{3,2,1,0:T(1,128)}), f32[128,5,1,128]{3,2,1,0:T(1,128)S(1)}, u32[]{:S(2)}, u32[]{:S(2)}) async-start(f32[128,5,1,128]{3,2,1,0:T(1,128)} %copy.36), calls=%async_computation.1 | async-start | bytes 655360 | tf_op jit(solution)/shard_map/all_to_all | solution.py:28
  39.4 0.0 all-gather.2.cloned.1.call-start
  39.5 0.7 all-gather.2.cloned.1.call-update
  40.9 15.5 %all-to-all-done.1 = f32[128,5,1,128]{3,2,1,0:T(1,128)S(1)} async-done(((f32[128,5,1,128]{3,2,1,0:T(1,128)}), f32[128,5,1,128]{3,2,1,0:T(1,128)S(1)}, u32[]{:S(2)}, u32[]{:S(2)}) %all-to-all-start.1) | async-done | bytes 327712 | tf_op jit(solution)/shard_map/all_to_all | solution.py:28
  56.4 0.1 reduce_sum.27
  56.5 0.0 copy-start.1
  56.6 0.1 subtract_convert_fusion.1
  56.6 0.1 subtract_convert_fusion
  56.7 0.1 maximum_bitcast_fusion
  56.8 0.2 fusion.19
  57.0 0.0 copy-done
  57.0 0.8 fusion.30
  57.8 0.2 fusion.16
  58.0 0.2 copy-done.1
  58.2 0.5 fusion.10
  58.6 0.7 broadcast_in_dim.63
  59.3 4.6 %all-to-all-start.2 = ((bf16[32,16,128]{2,1,0:T(8,128)(2,1)}), bf16[32,16,128]{2,1,0:T(8,128)(2,1)S(1)}, u32[]{:S(2)}, u32[]{:S(2)}) async-start(bf16[32,16,128]{2,1,0:T(8,128)(2,1)} %broadcast_in_dim.63), calls=%async_computation.2 | async-start | bytes 262144 | tf_op jit(solution)/shard_map/all_to_all | solution.py:28
  63.9 0.1 broadcast_in_dim.58
  64.0 11.2 %all-to-all-done.2 = bf16[32,16,128]{2,1,0:T(8,128)(2,1)S(1)} async-done(((bf16[32,16,128]{2,1,0:T(8,128)(2,1)}), bf16[32,16,128]{2,1,0:T(8,128)(2,1)S(1)}, u32[]{:S(2)}, u32[]{:S(2)}) %all-to-all-start.2) | async-done | bytes 131104 | tf_op jit(solution)/shard_map/all_to_all | solution.py:28
  75.2 0.0 all-gather.2.cloned.1.call-done
  75.2 0.1 broadcast_in_dim.64
  75.3 1.6 %convolution_bitcast_fusion.1 = f32[256,128]{0,1:T(8,128)S(1)} fusion(bf16[2048,256]{1,0:T(8,128)(2,1)} %all-gather.2.cloned.1.call-done, bf16[16,8,16,128]{3,2,1,0:T(8,128)(2,1)S(1)} %bitcast.47, pred[128]{0:T(512)(128)(4,1)S(1)} %broadcast_in_dim.58), kind=kOutput, calls=%fused_computation.6 | convolution fusion | flops 134479872 | bytes 1704064 | tf_op jit(solution)/shard_map/sk,kn->ns/dot_general | solution.py:87
  76.9 0.1 copy.42
  76.9 11.1 %all_to_all.20 = f32[16,16,128]{2,1,0:T(8,128)S(1)} all-to-all(f32[16,16,128]{2,1,0:T(8,128)S(1)} %bitcast.48), channel_id=1, replica_groups=mesh['gx'=32,'gy'=4,'gz'=4] {'gy','gz'}, dimensions={0} | all-to-all | bytes 262144 | tf_op jit(solution)/shard_map/all_to_all | solution.py:28
  88.1 0.6 reduce_sum.29
  (12 shorter events, 0.1 us)
Async XLA Ops:
  6.5 50.5 %copy-start = (bf16[1,4096,2,128]{3,2,1,0:T(2,128)(2,1)S(1)}, bf16[1,4096,2,128]{3,2,1,0:T(2,128)(2,1)}, u32[]{:S(2)}) copy-start(bf16[1,4096,2,128]{3,2,1,0:T(2,128)(2,1)} %param.8) | copy-start | bytes 6291460
  8.0 16.0 %all-to-all-start = ((bf16[16,16,128]{2,1,0:T(8,128)(2,1)}), bf16[16,16,128]{2,1,0:T(8,128)(2,1)S(1)}, u32[]{:S(2)}, u32[]{:S(2)}) async-start(bf16[16,16,128]{2,1,0:T(8,128)(2,1)} %broadcast_in_dim.60), calls=%async_computation | async-start | bytes 131072 | tf_op jit(solution)/shard_map/all_to_all | solution.py:28
  25.4 31.1 %all-to-all-start.1 = ((f32[128,5,1,128]{3,2,1,0:T(1,128)}), f32[128,5,1,128]{3,2,1,0:T(1,128)S(1)}, u32[]{:S(2)}, u32[]{:S(2)}) async-start(f32[128,5,1,128]{3,2,1,0:T(1,128)} %copy.36), calls=%async_computation.1 | async-start | bytes 655360 | tf_op jit(solution)/shard_map/all_to_all | solution.py:28
  39.4 35.8 %all-gather.2.cloned.1.call-start = ((), (), s32[]{:S(2)}) async-start(), calls=%async_computation.4 | async-start | bytes 1310720 | tf_op jit(solution)/shard_map/all_gather | solution.py:81
  56.5 1.7 %copy-start.1 = (bf16[1,4096,2,128]{3,2,1,0:T(2,128)(2,1)S(1)}, bf16[1,4096,2,128]{3,2,1,0:T(2,128)(2,1)}, u32[]{:S(2)}) copy-start(bf16[1,4096,2,128]{3,2,1,0:T(2,128)(2,1)} %param.9) | copy-start | bytes 6291460
  59.3 15.9 %all-to-all-start.2 = ((bf16[32,16,128]{2,1,0:T(8,128)(2,1)}), bf16[32,16,128]{2,1,0:T(8,128)(2,1)S(1)}, u32[]{:S(2)}, u32[]{:S(2)}) async-start(bf16[32,16,128]{2,1,0:T(8,128)(2,1)} %broadcast_in_dim.63), calls=%async_computation.2 | async-start | bytes 262144 | tf_op jit(solution)/shard_map/all_to_all | solution.py:28
Sparse Core Ops, SparseCore 0:
  42.4 28.1 all-gather.1

commit v2 on v0

v2 whole, which is shorter than its diff:
```python
import math

import jax
import jax.numpy as jnp
from jax import lax
from jax.experimental import pallas as pl
from jax.experimental.pallas import tpu as pltpu
from jax.sharding import Mesh
from jax.sharding import PartitionSpec as P

ROPE_BASE = 500000.0
LANES = 128
KEYS_STEP = 2048
EARLY = 3072
WIDTH = ("z", "yh")
GROUPS = ("yl", "core")
HEADS = GROUPS + ("x",)
SEQUENCES = WIDTH + ("x",)


def exchange(values, axes):
    return lax.all_to_all(values, axes, split_axis=0, concat_axis=0, tiled=True)


def load(values_ref, weights_ref, copies_ref, held_ref, first_ref, sems):
    weights = pltpu.make_async_copy(weights_ref, held_ref, sems.at[0])
    values = pltpu.make_async_copy(values_ref, first_ref, sems.at[1])
    values.start()
    weights.start()
    values.wait()
    copies_ref[...] = jnp.broadcast_to(first_ref[...][None], copies_ref.shape)
    weights.wait()


def in_hbm(values):
    return pltpu.with_memory_space_constraint(values, pltpu.HBM)


def fetch(
    length_ref,
    after_ref,
    keys_ref,
    values_ref,
    held_keys_ref,
    held_values_ref,
    turns_ref,
    sems,
):
    size = held_values_ref.shape[0]
    copies = [
        pltpu.make_async_copy(keys_ref, held_keys_ref, sems.at[0]),
        pltpu.make_async_copy(values_ref.at[pl.ds(0, size), :], held_values_ref, sems.at[1]),
    ]
    for copy in copies:
        copy.start()
    lane = lax.broadcasted_iota(jnp.int32, (8, LANES), 1)
    half = LANES // 2
    first = lane < half
    spot = jnp.where(first, lane, lane - half).astype(jnp.float32)
    freqs = jnp.exp(spot * (-2.0 * math.log(ROPE_BASE) / LANES))
    angles = length_ref[0].astype(jnp.float32) * freqs
    sine = jnp.sin(angles)
    turns_ref[0] = jnp.cos(angles)
    turns_ref[1] = jnp.where(first, -sine, sine)
    for copy in copies:
        copy.wait()


def project(mine_ref, weights_ref, out_ref, terms_ref):
    rows = mine_ref.shape[1]
    terms = lax.dot_general(
        mine_ref[...],
        weights_ref[...],
        (((0,), (0,)), ((), ())),
        preferred_element_type=jnp.float32,
    )
    pieces = terms.shape[1] // LANES
    for piece in range(pieces):
        terms_ref[pl.ds(piece * rows, rows), :] = terms[:, piece * LANES : (piece + 1) * LANES]
    deep, near = 8, 4
    wide = rows // deep
    for place in range(wide):
        first = (place // near) * deep * near + place % near
        for piece in range(pieces):
            out_ref[pl.ds(first * pieces + piece, deep, stride=near * pieces), :] = terms_ref[
                pl.ds(piece * rows + place, deep, stride=wide), :
            ]


def attend(
    length_ref,
    turns_ref,
    received_ref,
    keys_ref,
    early_ref,
    values_ref,
    out_ref,
    queries_ref,
    scores_ref,
    held_ref,
    sems,
):
    early = early_ref.shape[0]
    late = values_ref.shape[0] - early
    copies = [
        pltpu.make_async_copy(
            values_ref.at[pl.ds(early, late), :], held_ref.at[pl.ds(early, late), :], sems.at[0]
        ),
        pltpu.make_async_copy(early_ref, held_ref.at[pl.ds(0, early), :], sems.at[1]),
    ]
    for copy in copies:
        copy.start()
    groups = 2
    length = length_ref[0]
    blocks = 4
    rows = received_ref.shape[0] // 32
    pieces = rows // blocks
    heads = pieces - 1
    sums = jnp.sum(received_ref[...].reshape(16, 2 * rows, LANES), axis=0)
    mixed = sums[:rows] + sums[rows:]
    mixed = mixed.astype(jnp.bfloat16).astype(jnp.float32)
    turned = mixed * turns_ref[0, :1] + pltpu.roll(mixed, LANES // 2, 1) * turns_ref[1, :1]
    turned = turned.astype(jnp.bfloat16).astype(jnp.float32)
    for block in range(blocks):
        queries_ref[pl.ds(block * heads, heads), :] = turned[
            block * pieces : block * pieces + heads
        ]
    queries = queries_ref[...]

    def new(values, block):
        return values[block * pieces + heads : (block + 1) * pieces]

    scale = 1.0 / math.sqrt(LANES)
    row_group = lax.broadcasted_iota(jnp.int32, (4 * heads, 1), 0) // (2 * heads)
    key_new = jnp.where(row_group == 0, new(turned, 0), new(turned, 2))
    value_new = jnp.where(row_group == 0, new(mixed, 1), new(mixed, 3))
    own = jnp.sum(queries * key_new, axis=1, keepdims=True) * scale
    queries = queries.astype(jnp.bfloat16)
    span = keys_ref.shape[0]
    steps = span // KEYS_STEP
    column = lax.broadcasted_iota(jnp.int32, (4 * heads, KEYS_STEP), 1)
    same = (column % groups) == row_group
    place = jnp.where(same, column, groups * span)
    top = own
    for step in range(steps):
        block = pl.ds(step * KEYS_STEP, KEYS_STEP)
        scores = lax.dot_general(
            queries,
            keys_ref[block, :],
            (((1,), (1,)), ((), ())),
            preferred_element_type=jnp.float32,
        ) * scale
        scores = jnp.where(place < groups * length - step * KEYS_STEP, scores, -jnp.inf)
        scores_ref[:, block] = scores
        top = jnp.maximum(top, jnp.max(scores, axis=1, keepdims=True))
    own = jnp.exp(own - top)
    total = own
    for step in range(steps):
        block = pl.ds(step * KEYS_STEP, KEYS_STEP)
        exponent = jnp.exp(scores_ref[:, block] - top)
        scores_ref[:, block] = exponent
        total = total + jnp.sum(exponent, axis=1, keepdims=True)
    inverse = 1.0 / total
    own = (own * inverse).astype(jnp.bfloat16).astype(jnp.float32)
    attended = own * value_new
    for copy in copies:
        copy.wait()
    for step in range(steps):
        block = pl.ds(step * KEYS_STEP, KEYS_STEP)
        weights = (scores_ref[:, block] * inverse).astype(jnp.bfloat16)
        attended = attended + jnp.dot(
            weights, held_ref[block, :], preferred_element_type=jnp.float32
        )
    out_ref[...] = jnp.broadcast_to(attended.astype(jnp.bfloat16)[None], out_ref.shape)


def shards(activations, w_qkv, k_cache, v_cache, lengths, w_out):
    out_cols = w_qkv.shape[1]
    head_dim = k_cache.shape[3]
    rows = activations.shape[0]
    vmem = pl.BlockSpec(memory_space=pltpu.VMEM)
    hbm = pl.BlockSpec(memory_space=pltpu.HBM)
    anywhere = pl.BlockSpec(memory_space=pl.ANY)
    pieces = out_cols // head_dim
    copies, weights = pl.pallas_call(
        load,
        out_shape=(
            jax.ShapeDtypeStruct((16,) + activations.T.shape, activations.dtype),
            jax.ShapeDtypeStruct(w_qkv.shape, w_qkv.dtype),
        ),
        in_specs=[hbm, hbm],
        out_specs=(vmem, vmem),
        scratch_shapes=[
            pltpu.VMEM(activations.T.shape, activations.dtype),
            pltpu.SemaphoreType.DMA((2,)),
        ],
        compiler_params=pltpu.CompilerParams(vmem_limit_bytes=4 * 2**20),
    )(in_hbm(activations.T), in_hbm(w_qkv))
    mine_t = exchange(copies, HEADS)
    sent = pl.pallas_call(
        project,
        out_shape=jax.ShapeDtypeStruct((rows * pieces, head_dim), jnp.float32),
        in_specs=[vmem, vmem],
        out_specs=vmem,
        scratch_shapes=[pltpu.VMEM((rows * pieces, head_dim), jnp.float32)],
        compiler_params=pltpu.CompilerParams(vmem_limit_bytes=4 * 2**20),
    )(mine_t.reshape(-1, rows), weights)
    span = k_cache.shape[1] * k_cache.shape[2]
    cache = jax.ShapeDtypeStruct((span, head_dim), k_cache.dtype)
    early_cache = jax.ShapeDtypeStruct((EARLY, head_dim), v_cache.dtype)
    old_values = in_hbm(v_cache.reshape(span, head_dim))
    smem = pl.BlockSpec(memory_space=pltpu.SMEM)
    keys, early, turns = pl.pallas_call(
        fetch,
        out_shape=(cache, early_cache, jax.ShapeDtypeStruct((2, 8, LANES), jnp.float32)),
        in_specs=[smem, anywhere, hbm, hbm],
        out_specs=(vmem, vmem, vmem),
        scratch_shapes=[pltpu.SemaphoreType.DMA((2,))],
        compiler_params=pltpu.CompilerParams(vmem_limit_bytes=8 * 2**20),
        cost_estimate=pl.CostEstimate(
            flops=0, bytes_accessed=3 * span * head_dim, transcendentals=0
        ),
    )(lengths, sent, in_hbm(k_cache.reshape(span, head_dim)), old_values)
    received = exchange(sent.reshape(rows, pieces, 1, head_dim), ("yh", "z", "x"))
    heads = 16
    attended = pl.pallas_call(
        attend,
        out_shape=jax.ShapeDtypeStruct((32, heads, head_dim), jnp.bfloat16),
        in_specs=[smem, vmem, vmem, vmem, vmem, hbm],
        out_specs=vmem,
        scratch_shapes=[
            pltpu.VMEM((heads, head_dim), jnp.float32),
            pltpu.VMEM((heads, span), jnp.float32),
            pltpu.VMEM((span, head_dim), v_cache.dtype),
            pltpu.SemaphoreType.DMA((2,)),
        ],
        compiler_params=pltpu.CompilerParams(vmem_limit_bytes=8 * 2**20),
    )(lengths, turns, received.reshape(-1, head_dim), keys, early, old_values)
    head_rows = w_out.shape[0]
    heads = head_rows // head_dim
    mine = exchange(attended.reshape(rows, heads, head_dim), SEQUENCES)
    out_terms = jnp.einsum(
        "shd,hdn->ns",
        mine,
        w_out.reshape(heads, head_dim, -1),
        preferred_element_type=jnp.float32,
    )
    out_parts = exchange(out_terms.reshape(16, -1, rows), HEADS)
    return jnp.sum(out_parts, axis=0).astype(jnp.bfloat16).T


def solution(mesh):
    split = Mesh(mesh.devices.reshape(8, 4, 2, 2, 4), ("z", "yh", "yl", "core", "x"))
    placed = (
        P(None, WIDTH + HEADS),
        P(WIDTH, HEADS),
        P(SEQUENCES, None, GROUPS, None),
        P(SEQUENCES, None, GROUPS, None),
        P(SEQUENCES),
        P(HEADS, WIDTH),
    )
    return jax.shard_map(
        shards, mesh=split, in_specs=placed, out_specs=P(None, WIDTH + HEADS), check_vma=False
    )
```

time: 658 us -> 83.1 us (0.13)
  blocking collectives: 487 us -> 46.6 us
  waiting for transfers between devices: 143 us -> 14.2 us
  between operations: 14.8 us -> 0.7 us
  starting transfers between devices: 3.54 us -> 14.7 us
    all_gather x2 -> x0, blocking collectives: 349 us -> none  [the longest x1 318 us: shards(): lax.all_gather(attended_row, ('gx', 'gz'), axis=0, tiled=True)]
    reduce_scatter x1 -> x0, waiting for transfers between devices: 139 us -> none  [shards(): lax.psum_scatter(out_terms, ('gy', 'gz'), scatter_dimension=1, tiled=True)]
    unnamed x1 -> x0, blocking collectives: 137 us -> none
    all_to_all x0 -> x3, blocking collectives: none -> 46.6 us  [exchange(): return lax.all_to_all(values, axes, split_axis=0, concat_axis=0, tiled=True)]
    all_to_all x1, starting transfers between devices: 3.54 us -> 14.7 us  [exchange(): return lax.all_to_all(values, axes, split_axis=0, concat_axis=0, tiled=True)]
    all_to_all x1, waiting for transfers between devices: 3.72 us -> 14.2 us  [exchange(): return lax.all_to_all(values, axes, split_axis=0, concat_axis=0, tiled=True)]
  transfers between devices with their start and end apart: 2 -> 1, of which waited for: 2 -> 1; matrix products, arithmetic and copies ran while one was open for 0% -> 0% of each run, Pallas kernels for 0% -> 2%
where the time goes in v2:
time: 83.1 us; the launch traced here: 82.8 us
  blocking collectives  46.6 us (56%)
  starting transfers between devices  14.7 us (18%)
  waiting for transfers between devices  14.2 us (17%)
  Pallas kernels  5.61 us (7%)
    all_to_all x3, blocking collectives, exchange(): return lax.all_to_all(values, axes, split_axis=0, concat_axis=0, tiled=True)  46.6 us
    all_to_all x1, starting transfers between devices, exchange(): return lax.all_to_all(values, axes, split_axis=0, concat_axis=0, tiled=True)  14.7 us
    all_to_all x1, waiting for transfers between devices, exchange(): return lax.all_to_all(values, axes, split_axis=0, concat_axis=0, tiled=True)  14.2 us
    pallas_call x1, Pallas kernels, shards(): pl.pallas_call(fetch, out_shape=(cache, early_cache, jax.ShapeDtypeStruct...  1.79 us
    pallas_call x1, Pallas kernels, shards(): pl.pallas_call(attend, out_shape=jax.ShapeDtypeStruct((32, heads, head_di...  1.74 us
  transfers between devices with their start and end apart: 1, of which 1 were waited for; matrix products, arithmetic and copies ran while one was open for 0% of the time, Pallas kernels for 2%

profile of v2, /device:TPU:1, one launch (start us, length us, event | category | flops | bytes accessed | tf_op | source)
XLA Modules:
  0.0 82.8 jit_solution(6275144968278788590)
XLA Ops:
  0.0 0.0 copy-start
  0.0 1.0 %shard_map.64 = (bf16[16,16,128]{2,1,0:T(8,128)(2,1)S(1)}, bf16[256,640]{1,0:T(8,128)(2,1)S(1)}) custom-call(bf16[16,128]{1,0:T(8,128)(2,1)} %bitcast.25, bf16[256,640]{1,0:T(8,128)(2,1)} %weights_ref.1), custom_call_target="tpu_custom_call" | custom-call | tf_op jit(solution)/shard_map/pallas_call | solution.py:185
  1.1 15.2 %all_to_all.20 = bf16[16,16,128]{2,1,0:T(8,128)(2,1)S(1)} all-to-all(bf16[16,16,128]{2,1,0:T(8,128)(2,1)S(1)} %get-tuple-element.10), channel_id=1, replica_groups=mesh['z'=8,'yh'=4,'yl'=2,'core'=2,'x'=4] {'yl','core','x'}, dimensions={0} | all-to-all | bytes 131072 | tf_op jit(solution)/shard_map/all_to_all | solution.py:22
  16.2 1.0 %shard_map.65.after_ref = f32[640,128]{1,0:T(8,128)} custom-call(bf16[256,128]{1,0:T(8,128)(2,1)S(1)} %bitcast.20, bf16[256,640]{1,0:T(8,128)(2,1)S(1)} %get-tuple-element.11.weights_ref), custom_call_target="tpu_custom_call" | custom-call | tf_op jit(solution)/shard_map/pallas_call | solution.py:200
  17.3 14.7 %all-to-all-start.1 = ((f32[128,5,1,128]{3,2,1,0:T(1,128)}), f32[128,5,1,128]{3,2,1,0:T(1,128)S(1)}, u32[]{:S(2)}, u32[]{:S(2)}) async-start(f32[128,5,1,128]{3,2,1,0:T(1,128)} %bitcast.4), calls=%async_computation.1 | async-start | bytes 655360 | tf_op jit(solution)/shard_map/all_to_all | solution.py:22
  32.7 1.8 %shard_map.66 = (bf16[8192,128]{1,0:T(8,128)(2,1)S(1)}, bf16[3072,128]{1,0:T(8,128)(2,1)S(1)}, f32[2,8,128]{2,1,0:T(8,128)S(1)}) custom-call(s32[1]{0:T(128)S(6)} %copy.15.length_ref, f32[640,128]{1,0:T(8,128)} %shard_map.65.after_ref, bf16[8192,128]{1,0:T(8,128)(2,1)} %bitcast.23, bf16[8192,128]{1,0:T(8,128)(2,1)} %bitcast.21), custom_call_target="tpu_custom_call" | custom-call | bytes 3145728 | tf_op jit(solution)/shard_map/pallas_call | solution.py:213
  34.4 14.2 %all-to-all-done.1 = f32[128,5,1,128]{3,2,1,0:T(1,128)S(1)} async-done(((f32[128,5,1,128]{3,2,1,0:T(1,128)}), f32[128,5,1,128]{3,2,1,0:T(1,128)S(1)}, u32[]{:S(2)}, u32[]{:S(2)}) %all-to-all-start.1) | async-done | bytes 327712 | tf_op jit(solution)/shard_map/all_to_all | solution.py:22
  48.6 1.7 %shard_map.67 = bf16[32,16,128]{2,1,0:T(8,128)(2,1)S(1)} custom-call(s32[1]{0:T(128)S(6)} %copy.15.length_ref, f32[2,8,128]{2,1,0:T(8,128)S(1)} %get-tuple-element.12.turns_ref, f32[640,128]{1,0:T(8,128)S(1)} %bitcast.18, bf16[8192,128]{1,0:T(8,128)(2,1)S(1)} %get-tuple-element.13.keys_ref, bf16[3072,128]{1,0:T(8,128)(2,1)S(1)} %get-tuple-element.14.early_ref, ...), custom_call_target="tpu_custom_call" | custom-call | tf_op jit(solution)/shard_map/pallas_call | solution.py:226
  50.4 20.5 %all_to_all.21 = bf16[128,4,128]{2,1,0:T(4,128)(2,1)S(1)} all-to-all(bf16[128,4,128]{2,1,0:T(4,128)(2,1)S(1)} %bitcast.19), channel_id=1, replica_groups=mesh['z'=8,'yh'=4,'yl'=2,'core'=2,'x'=4] {'z','yh','x'}, dimensions={0} | all-to-all | bytes 262144 | tf_op jit(solution)/shard_map/all_to_all | solution.py:22
  70.9 0.0 copy-done
  70.9 0.2 convolution_bitcast_fusion
  71.1 0.1 copy.12
  71.2 10.9 %all_to_all.22 = f32[16,16,128]{2,1,0:T(8,128)S(1)} all-to-all(f32[16,16,128]{2,1,0:T(8,128)S(1)} %bitcast.24), channel_id=1, replica_groups=mesh['z'=8,'yh'=4,'yl'=2,'core'=2,'x'=4] {'yl','core','x'}, dimensions={0} | all-to-all | bytes 262144 | tf_op jit(solution)/shard_map/all_to_all | solution.py:22
  82.2 0.6 reduce_sum.9
Async XLA Ops:
  0.0 70.9 %copy-start = (bf16[512,256]{1,0:T(8,128)(2,1)S(1)}, bf16[512,256]{1,0:T(8,128)(2,1)}, u32[]{:S(2)}) copy-start(bf16[512,256]{1,0:T(8,128)(2,1)} %param.11) | copy-start | bytes 786436
  17.3 31.4 %all-to-all-start.1 = ((f32[128,5,1,128]{3,2,1,0:T(1,128)}), f32[128,5,1,128]{3,2,1,0:T(1,128)S(1)}, u32[]{:S(2)}, u32[]{:S(2)}) async-start(f32[128,5,1,128]{3,2,1,0:T(1,128)} %bitcast.4), calls=%async_computation.1 | async-start | bytes 655360 | tf_op jit(solution)/shard_map/all_to_all | solution.py:22

commit v3 on v2

--- a/solution.py
+++ b/solution.py
@@ -11,11 +11,12 @@
 ROPE_BASE = 500000.0
 LANES = 128
 KEYS_STEP = 2048
-EARLY = 3072
+EARLY = 4096
 WIDTH = ("z", "yh")
 GROUPS = ("yl", "core")
-HEADS = GROUPS + ("x",)
-SEQUENCES = WIDTH + ("x",)
+ACROSS = ("xa", "xb")
+HEADS = GROUPS + ACROSS
+SEQUENCES = WIDTH + ACROSS
 
 
 def exchange(values, axes):
@@ -89,6 +90,7 @@
 
 def attend(
     length_ref,
+    half_ref,
     turns_ref,
     received_ref,
     keys_ref,
@@ -171,7 +173,39 @@
         attended = attended + jnp.dot(
             weights, held_ref[block, :], preferred_element_type=jnp.float32
         )
-    out_ref[...] = jnp.broadcast_to(attended.astype(jnp.bfloat16)[None], out_ref.shape)
+    size = attended.shape[0] // 4
+    block = [attended[i * size : (i + 1) * size] for i in range(4)]
+    lower = jnp.concatenate([block[0], block[3], block[1], block[2]], axis=0)
+    upper = jnp.concatenate([block[2], block[1], block[3], block[0]], axis=0)
+    ordered = jnp.where(half_ref[0] == 0, lower, upper).astype(jnp.bfloat16)
+    out_ref[...] = jnp.broadcast_to(ordered[None], out_ref.shape)
+
+
+def finish(half_ref, first_ref, received_ref, weights_ref, out_ref, rows_ref):
+    heads = weights_ref.shape[0] // LANES
+    count = first_ref.shape[0]
+    rows_ref[...] = received_ref[...].astype(jnp.float32)
+    ours = jnp.concatenate(
+        [
+            rows_ref[pl.ds(heads + head, count, stride=2 * heads), :]
+            for head in range(heads)
+        ],
+        axis=1,
+    ).astype(jnp.bfloat16)
+    sequence = lax.broadcasted_iota(jnp.int32, (count, 2 * count), 1)
+    source = lax.broadcasted_iota(jnp.int32, (count, 2 * count), 0)
+    place = source + 2 * (source // 2) + 2 * half_ref[0]
+    chosen = (sequence == place).astype(jnp.float32)
+    terms = first_ref[...] + jnp.dot(
+        ours, weights_ref[...], preferred_element_type=jnp.float32
+    )
+    out_ref[...] = lax.dot_general(
+        terms,
+        chosen,
+        (((0,), (0,)), ((), ())),
+        precision=lax.Precision.HIGHEST,
+        preferred_element_type=jnp.float32,
+    )
 
 
 def shards(activations, w_qkv, k_cache, v_cache, lengths, w_out):
@@ -221,12 +255,15 @@
             flops=0, bytes_accessed=3 * span * head_dim, transcendentals=0
         ),
     )(lengths, sent, in_hbm(k_cache.reshape(span, head_dim)), old_values)
-    received = exchange(sent.reshape(rows, pieces, 1, head_dim), ("yh", "z", "x"))
+    received = exchange(sent.reshape(rows, pieces, 1, head_dim), ("yh", "z") + ACROSS)
+    w_late, _ = lax.optimization_barrier((w_out, sent))
+    w_other = lax.ppermute(w_late, ACROSS, [(i, 3 - i) for i in range(4)])
+    half = lax.axis_index("xa").reshape(1)
     heads = 16
     attended = pl.pallas_call(
         attend,
         out_shape=jax.ShapeDtypeStruct((32, heads, head_dim), jnp.bfloat16),
-        in_specs=[smem, vmem, vmem, vmem, vmem, hbm],
+        in_specs=[smem, smem, vmem, vmem, vmem, vmem, hbm],
         out_specs=vmem,
         scratch_shapes=[
             pltpu.VMEM((heads, head_dim), jnp.float32),
@@ -235,22 +272,31 @@
             pltpu.SemaphoreType.DMA((2,)),
         ],
         compiler_params=pltpu.CompilerParams(vmem_limit_bytes=8 * 2**20),
-    )(lengths, turns, received.reshape(-1, head_dim), keys, early, old_values)
-    head_rows = w_out.shape[0]
-    heads = head_rows // head_dim
-    mine = exchange(attended.reshape(rows, heads, head_dim), SEQUENCES)
-    out_terms = jnp.einsum(
-        "shd,hdn->ns",
-        mine,
-        w_out.reshape(heads, head_dim, -1),
+    )(lengths, half, turns, received.reshape(-1, head_dim), keys, early, old_values)
+    near = WIDTH + ("xb",)
+    mine = exchange(attended.reshape(rows // 2, heads // 2, head_dim), near)
+    own_terms = jnp.einsum(
+        "shd,hdn->sn",
+        mine[:, : heads // 4],
+        w_out.reshape(heads // 4, head_dim, -1),
         preferred_element_type=jnp.float32,
     )
+    out_terms = pl.pallas_call(
+        finish,
+        out_shape=jax.ShapeDtypeStruct((w_out.shape[1], rows), jnp.float32),
+        in_specs=[smem, vmem, vmem, vmem],
+        out_specs=vmem,
+        scratch_shapes=[pltpu.VMEM((rows * 4, head_dim), jnp.float32)],
+        compiler_params=pltpu.CompilerParams(vmem_limit_bytes=4 * 2**20),
+    )(half, own_terms, mine.reshape(-1, head_dim), w_other)
     out_parts = exchange(out_terms.reshape(16, -1, rows), HEADS)
     return jnp.sum(out_parts, axis=0).astype(jnp.bfloat16).T
 
 
 def solution(mesh):
-    split = Mesh(mesh.devices.reshape(8, 4, 2, 2, 4), ("z", "yh", "yl", "core", "x"))
+    split = Mesh(
+        mesh.devices.reshape(8, 4, 2, 2, 2, 2), ("z", "yh", "yl", "core", "xa", "xb")
+    )
     placed = (
         P(None, WIDTH + HEADS),
         P(WIDTH, HEADS),

time: 83.1 us -> 83 us (level)
  blocking collectives: 46.6 us -> 27 us
  starting transfers between devices: 14.7 us -> 23.5 us
  waiting for transfers between devices: 14.2 us -> 22.9 us
  matrix products: 0.19 us -> 1.12 us
    all_to_all x3 -> x2, blocking collectives: 46.6 us -> 27 us  [exchange(): return lax.all_to_all(values, axes, split_axis=0, concat_axis=0, tiled=True)]
    all_to_all x1 -> x2, waiting for transfers between devices: 14.2 us -> 22.9 us  [exchange(): return lax.all_to_all(values, axes, split_axis=0, concat_axis=0, tiled=True)]
    all_to_all x1 -> x2, starting transfers between devices: 14.7 us -> 20 us  [exchange(): return lax.all_to_all(values, axes, split_axis=0, concat_axis=0, tiled=True)]
    ppermute x0 -> x1, starting transfers between devices: none -> 3.45 us  [shards(): w_other = lax.ppermute(w_late, ACROSS, [(i, 3 - i) for i in range(4)])]
    dot_general x1, matrix products: 0.19 us -> 1.12 us  [shards(): jnp.einsum('shd,hdn->sn', mine[:, :heads // 4], w_out.reshape(heads // 4,...]
  transfers between devices with their start and end apart: 1 -> 3, of which waited for: 1 -> 2; matrix products, arithmetic and copies ran while one was open for 0% -> 1% of each run, Pallas kernels for 2% -> 2%
where the time goes in v3:
time: 83 us; the launch traced here: 82.6 us
  blocking collectives  27 us (33%)
  starting transfers between devices  23.5 us (28%)
  waiting for transfers between devices  22.9 us (28%)
  Pallas kernels  6.1 us (7%)
  matrix products  1.12 us (1%)
    all_to_all x2, blocking collectives, exchange(): return lax.all_to_all(values, axes, split_axis=0, concat_axis=0, tiled=True)  27 us
    all_to_all x2, waiting for transfers between devices, exchange(): return lax.all_to_all(values, axes, split_axis=0, concat_axis=0, tiled=True)  22.9 us
    all_to_all x2, starting transfers between devices, exchange(): return lax.all_to_all(values, axes, split_axis=0, concat_axis=0, tiled=True)  20 us
    ppermute x1, starting transfers between devices, shards(): w_other = lax.ppermute(w_late, ACROSS, [(i, 3 - i) for i in range(4)])  3.45 us
    pallas_call x1, Pallas kernels, shards(): pl.pallas_call(fetch, out_shape=(cache, early_cache, jax.ShapeDtypeStruct...  1.88 us
  transfers between devices with their start and end apart: 3, of which 2 were waited for; matrix products, arithmetic and copies ran while one was open for 1% of the time, Pallas kernels for 2%

profile of v3, /device:TPU:1, one launch (start us, length us, event | category | flops | bytes accessed | tf_op | source)
XLA Modules:
  0.0 82.6 jit_solution(17786185678052710858)
XLA Ops:
  0.0 1.0 %shard_map.64 = (bf16[16,16,128]{2,1,0:T(8,128)(2,1)S(1)}, bf16[256,640]{1,0:T(8,128)(2,1)S(1)}) custom-call(bf16[16,128]{1,0:T(8,128)(2,1)} %bitcast.26, bf16[256,640]{1,0:T(8,128)(2,1)} %weights_ref.1), custom_call_target="tpu_custom_call" | custom-call | tf_op jit(solution)/shard_map/pallas_call | solution.py:219
  1.0 15.2 %all_to_all.20 = bf16[16,16,128]{2,1,0:T(8,128)(2,1)S(1)} all-to-all(bf16[16,16,128]{2,1,0:T(8,128)(2,1)S(1)} %get-tuple-element.11), channel_id=1, replica_groups=mesh['z'=8,'yh'=4,'yl'=2,'core'=2,'xa'=2,'xb'=2] {'yl','core','xa','xb'}, dimensions={0} | all-to-all | bytes 131072 | tf_op jit(solution)/shard_map/all_to_all | solution.py:23
  16.2 1.0 %shard_map.65.after_ref = f32[640,128]{1,0:T(8,128)} custom-call(bf16[256,128]{1,0:T(8,128)(2,1)S(1)} %bitcast.21, bf16[256,640]{1,0:T(8,128)(2,1)S(1)} %get-tuple-element.12.weights_ref), custom_call_target="tpu_custom_call" | custom-call | tf_op jit(solution)/shard_map/pallas_call | solution.py:234
  17.2 14.7 %all-to-all-start.1 = ((f32[128,5,1,128]{3,2,1,0:T(1,128)}), f32[128,5,1,128]{3,2,1,0:T(1,128)S(1)}, u32[]{:S(2)}, u32[]{:S(2)}) async-start(f32[128,5,1,128]{3,2,1,0:T(1,128)} %bitcast.5), calls=%async_computation.1 | async-start | bytes 655360 | tf_op jit(solution)/shard_map/all_to_all | solution.py:23
  32.6 1.9 %shard_map.66 = (bf16[8192,128]{1,0:T(8,128)(2,1)S(1)}, bf16[4096,128]{1,0:T(8,128)(2,1)S(1)}, f32[2,8,128]{2,1,0:T(8,128)S(1)}) custom-call(s32[1]{0:T(128)S(6)} %copy.16.length_ref, f32[640,128]{1,0:T(8,128)} %shard_map.65.after_ref, bf16[8192,128]{1,0:T(8,128)(2,1)} %bitcast.24, bf16[8192,128]{1,0:T(8,128)(2,1)} %bitcast.22), custom_call_target="tpu_custom_call" | custom-call | bytes 3145728 | tf_op jit(solution)/shard_map/pallas_call | solution.py:247
  34.5 14.1 %all-to-all-done.1 = f32[128,5,1,128]{3,2,1,0:T(1,128)S(1)} async-done(((f32[128,5,1,128]{3,2,1,0:T(1,128)}), f32[128,5,1,128]{3,2,1,0:T(1,128)S(1)}, u32[]{:S(2)}, u32[]{:S(2)}) %all-to-all-start.1) | async-done | bytes 327712 | tf_op jit(solution)/shard_map/all_to_all | solution.py:23
  48.6 1.6 %shard_map.67 = bf16[32,16,128]{2,1,0:T(8,128)(2,1)S(1)} custom-call(s32[1]{0:T(128)S(6)} %copy.16.length_ref, s32[1]{0:T(128)} %bitcast.half_ref, f32[2,8,128]{2,1,0:T(8,128)S(1)} %get-tuple-element.13.turns_ref, f32[640,128]{1,0:T(8,128)S(1)} %bitcast.17, bf16[8192,128]{1,0:T(8,128)(2,1)S(1)} %get-tuple-element.14.keys_ref, ...), custom_call_target="tpu_custom_call" | custom-call | tf_op jit(solution)/shard_map/pallas_call | solution.py:263
  50.2 0.0 copy-start
  50.3 0.6 copy-done
  50.9 5.3 %all-to-all-start.2 = ((bf16[64,8,128]{2,1,0:T(8,128)(2,1)}), bf16[64,8,128]{2,1,0:T(8,128)(2,1)S(1)}, u32[]{:S(2)}, u32[]{:S(2)}) async-start(bf16[64,8,128]{2,1,0:T(8,128)(2,1)} %bitcast.19), calls=%async_computation.2 | async-start | bytes 262144 | tf_op jit(solution)/shard_map/all_to_all | solution.py:23
  56.2 3.4 %collective-permute-start = (bf16[512,256]{1,0:T(8,128)(2,1)}, bf16[512,256]{1,0:T(8,128)(2,1)S(1)}, u32[]{:S(2)}, u32[]{:S(2)}) collective-permute-start(bf16[512,256]{1,0:T(8,128)(2,1)} %param.11), channel_id=1, source_target_pairs={{0,3},{1,2},{2,1},{3,0},{4,7},{5,6},{6,5},{7,4},{8,11},{9,10},{10,... | collective-permute-start | bytes 786440 | tf_op jit(solution)/shard_map/ppermute | solution.py:260
  59.6 8.8 %all-to-all-done.2 = bf16[64,8,128]{2,1,0:T(8,128)(2,1)S(1)} async-done(((bf16[64,8,128]{2,1,0:T(8,128)(2,1)}), bf16[64,8,128]{2,1,0:T(8,128)(2,1)S(1)}, u32[]{:S(2)}, u32[]{:S(2)}) %all-to-all-start.2) | async-done | bytes 131104 | tf_op jit(solution)/shard_map/all_to_all | solution.py:23
  68.4 1.1 %convolution_bitcast_fusion.first_ref = f32[64,256]{1,0:T(8,128)S(1)} fusion(bf16[4,128,256]{2,1,0:T(8,128)(2,1)} %bitcast.25, bf16[64,4,128]{2,1,0:T(4,128)(2,1)S(1)} %slice.4), kind=kOutput, calls=%fused_computation | convolution fusion | flops 16777216 | bytes 393216 | tf_op jit(solution)/shard_map/shd,hdn->sn/dot_general | solution.py:278
  69.6 0.0 collective-permute-done.weights_ref
  69.6 0.5 shard_map.68
  70.1 11.9 %all_to_all.21 = f32[16,16,128]{2,1,0:T(8,128)S(1)} all-to-all(f32[16,16,128]{2,1,0:T(8,128)S(1)} %bitcast.20), channel_id=1, replica_groups=mesh['z'=8,'yh'=4,'yl'=2,'core'=2,'xa'=2,'xb'=2] {'yl','core','xa','xb'}, dimensions={0} | all-to-all | bytes 262144 | tf_op jit(solution)/shard_map/all_to_all | solution.py:23
  82.0 0.6 reduce_sum.9
  (1 shorter events, 0.0 us)
Async XLA Ops:
  17.2 31.4 %all-to-all-start.1 = ((f32[128,5,1,128]{3,2,1,0:T(1,128)}), f32[128,5,1,128]{3,2,1,0:T(1,128)S(1)}, u32[]{:S(2)}, u32[]{:S(2)}) async-start(f32[128,5,1,128]{3,2,1,0:T(1,128)} %bitcast.5), calls=%async_computation.1 | async-start | bytes 655360 | tf_op jit(solution)/shard_map/all_to_all | solution.py:23
  50.2 0.6 copy-start
  50.9 17.5 %all-to-all-start.2 = ((bf16[64,8,128]{2,1,0:T(8,128)(2,1)}), bf16[64,8,128]{2,1,0:T(8,128)(2,1)S(1)}, u32[]{:S(2)}, u32[]{:S(2)}) async-start(bf16[64,8,128]{2,1,0:T(8,128)(2,1)} %bitcast.19), calls=%async_computation.2 | async-start | bytes 262144 | tf_op jit(solution)/shard_map/all_to_all | solution.py:23
  56.2 13.4 %collective-permute-start = (bf16[512,256]{1,0:T(8,128)(2,1)}, bf16[512,256]{1,0:T(8,128)(2,1)S(1)}, u32[]{:S(2)}, u32[]{:S(2)}) collective-permute-start(bf16[512,256]{1,0:T(8,128)(2,1)} %param.11), channel_id=1, source_target_pairs={{0,3},{1,2},{2,1},{3,0},{4,7},{5,6},{6,5},{7,4},{8,11},{9,10},{10,... | collective-permute-start | bytes 786440 | tf_op jit(solution)/shard_map/ppermute | solution.py:260

commit v4 on v3

--- a/solution.py
+++ b/solution.py
@@ -11,7 +11,7 @@
 ROPE_BASE = 500000.0
 LANES = 128
 KEYS_STEP = 2048
-EARLY = 4096
+EARLY = 3072
 WIDTH = ("z", "yh")
 GROUPS = ("yl", "core")
 ACROSS = ("xa", "xb")

time: 83 us -> 82.2 us (level)
  matrix products: 1.12 us -> 0.17 us
    dot_general x1, matrix products: 1.12 us -> 0.17 us  [shards(): jnp.einsum('shd,hdn->sn', mine[:, :heads // 4], w_out.reshape(heads // 4,...]
  transfers between devices with their start and end apart: 3 -> 3, of which waited for: 2 -> 2; matrix products, arithmetic and copies ran while one was open for 1% -> 0% of each run, Pallas kernels for 2% -> 2%
where the time goes in v4:
time: 82.2 us; the launch traced here: 81.8 us
  blocking collectives  27 us (33%)
  starting transfers between devices  23.5 us (29%)
  waiting for transfers between devices  23 us (28%)
  Pallas kernels  6.79 us (8%)
    all_to_all x2, blocking collectives, exchange(): return lax.all_to_all(values, axes, split_axis=0, concat_axis=0, tiled=True)  27 us
    all_to_all x2, waiting for transfers between devices, exchange(): return lax.all_to_all(values, axes, split_axis=0, concat_axis=0, tiled=True)  23 us
    all_to_all x2, starting transfers between devices, exchange(): return lax.all_to_all(values, axes, split_axis=0, concat_axis=0, tiled=True)  20 us
    ppermute x1, starting transfers between devices, shards(): w_other = lax.ppermute(w_late, ACROSS, [(i, 3 - i) for i in range(4)])  3.45 us
    pallas_call x1, Pallas kernels, shards(): pl.pallas_call(attend, out_shape=jax.ShapeDtypeStruct((32, heads, head_di...  2.43 us
    pallas_call x1, Pallas kernels, shards(): pl.pallas_call(fetch, out_shape=(cache, early_cache, jax.ShapeDtypeStruct...  1.79 us
  transfers between devices with their start and end apart: 3, of which 2 were waited for; matrix products, arithmetic and copies ran while one was open for 0% of the time, Pallas kernels for 2%

profile of v4, /device:TPU:1, one launch (start us, length us, event | category | flops | bytes accessed | tf_op | source)
XLA Modules:
  0.0 81.8 jit_solution(15100342364050277803)
XLA Ops:
  0.0 1.0 %shard_map.64 = (bf16[16,16,128]{2,1,0:T(8,128)(2,1)S(1)}, bf16[256,640]{1,0:T(8,128)(2,1)S(1)}) custom-call(bf16[16,128]{1,0:T(8,128)(2,1)} %bitcast.25, bf16[256,640]{1,0:T(8,128)(2,1)} %weights_ref.1), custom_call_target="tpu_custom_call" | custom-call | tf_op jit(solution)/shard_map/pallas_call | solution.py:219
  1.0 15.2 %all_to_all.20 = bf16[16,16,128]{2,1,0:T(8,128)(2,1)S(1)} all-to-all(bf16[16,16,128]{2,1,0:T(8,128)(2,1)S(1)} %get-tuple-element.11), channel_id=1, replica_groups=mesh['z'=8,'yh'=4,'yl'=2,'core'=2,'xa'=2,'xb'=2] {'yl','core','xa','xb'}, dimensions={0} | all-to-all | bytes 131072 | tf_op jit(solution)/shard_map/all_to_all | solution.py:23
  16.2 1.0 %shard_map.65.after_ref = f32[640,128]{1,0:T(8,128)} custom-call(bf16[256,128]{1,0:T(8,128)(2,1)S(1)} %bitcast.20, bf16[256,640]{1,0:T(8,128)(2,1)S(1)} %get-tuple-element.12.weights_ref), custom_call_target="tpu_custom_call" | custom-call | tf_op jit(solution)/shard_map/pallas_call | solution.py:234
  17.2 14.7 %all-to-all-start.1 = ((f32[128,5,1,128]{3,2,1,0:T(1,128)}), f32[128,5,1,128]{3,2,1,0:T(1,128)S(1)}, u32[]{:S(2)}, u32[]{:S(2)}) async-start(f32[128,5,1,128]{3,2,1,0:T(1,128)} %bitcast.5), calls=%async_computation.1 | async-start | bytes 655360 | tf_op jit(solution)/shard_map/all_to_all | solution.py:23
  32.6 1.8 %shard_map.66 = (bf16[8192,128]{1,0:T(8,128)(2,1)S(1)}, bf16[3072,128]{1,0:T(8,128)(2,1)S(1)}, f32[2,8,128]{2,1,0:T(8,128)S(1)}) custom-call(s32[1]{0:T(128)S(6)} %copy.16.length_ref, f32[640,128]{1,0:T(8,128)} %shard_map.65.after_ref, bf16[8192,128]{1,0:T(8,128)(2,1)} %bitcast.23, bf16[8192,128]{1,0:T(8,128)(2,1)} %bitcast.21), custom_call_target="tpu_custom_call" | custom-call | bytes 3145728 | tf_op jit(solution)/shard_map/pallas_call | solution.py:247
  34.4 14.2 %all-to-all-done.1 = f32[128,5,1,128]{3,2,1,0:T(1,128)S(1)} async-done(((f32[128,5,1,128]{3,2,1,0:T(1,128)}), f32[128,5,1,128]{3,2,1,0:T(1,128)S(1)}, u32[]{:S(2)}, u32[]{:S(2)}) %all-to-all-start.1) | async-done | bytes 327712 | tf_op jit(solution)/shard_map/all_to_all | solution.py:23
  48.6 0.0 copy-start
  48.6 2.4 %shard_map.67 = bf16[32,16,128]{2,1,0:T(8,128)(2,1)} custom-call(s32[1]{0:T(128)S(6)} %copy.16.length_ref, s32[1]{0:T(128)} %bitcast.half_ref, f32[2,8,128]{2,1,0:T(8,128)S(1)} %get-tuple-element.13.turns_ref, f32[640,128]{1,0:T(8,128)S(1)} %bitcast.17, bf16[8192,128]{1,0:T(8,128)(2,1)S(1)} %get-tuple-element.14.keys_ref, ...), custom_call_target="tpu_custom_call" | custom-call | tf_op jit(solution)/shard_map/pallas_call | solution.py:263
  51.0 5.3 %all-to-all-start.2 = ((bf16[64,8,128]{2,1,0:T(8,128)(2,1)}), bf16[64,8,128]{2,1,0:T(8,128)(2,1)S(1)}, u32[]{:S(2)}, u32[]{:S(2)}) async-start(bf16[64,8,128]{2,1,0:T(8,128)(2,1)} %bitcast.7), calls=%async_computation.2 | async-start | bytes 262144 | tf_op jit(solution)/shard_map/all_to_all | solution.py:23
  56.3 0.0 copy-done
  56.3 3.4 %collective-permute-start = (bf16[512,256]{1,0:T(8,128)(2,1)S(1)}, bf16[512,256]{1,0:T(8,128)(2,1)S(1)}, u32[]{:S(2)}, u32[]{:S(2)}) collective-permute-start(bf16[512,256]{1,0:T(8,128)(2,1)S(1)} %copy-done), channel_id=1, source_target_pairs={{0,3},{1,2},{2,1},{3,0},{4,7},{5,6},{6,5},{7,4},{8,11},{9,10},{10,... | collective-permute-start | bytes 786440 | tf_op jit(solution)/shard_map/ppermute | solution.py:260
  59.8 8.8 %all-to-all-done.2 = bf16[64,8,128]{2,1,0:T(8,128)(2,1)S(1)} async-done(((bf16[64,8,128]{2,1,0:T(8,128)(2,1)}), bf16[64,8,128]{2,1,0:T(8,128)(2,1)S(1)}, u32[]{:S(2)}, u32[]{:S(2)}) %all-to-all-start.2) | async-done | bytes 131104 | tf_op jit(solution)/shard_map/all_to_all | solution.py:23
  68.6 0.2 convolution_bitcast_fusion.first_ref
  68.8 0.0 collective-permute-done.weights_ref
  68.8 0.5 shard_map.68
  69.3 11.9 %all_to_all.21 = f32[16,16,128]{2,1,0:T(8,128)S(1)} all-to-all(f32[16,16,128]{2,1,0:T(8,128)S(1)} %bitcast.19), channel_id=1, replica_groups=mesh['z'=8,'yh'=4,'yl'=2,'core'=2,'xa'=2,'xb'=2] {'yl','core','xa','xb'}, dimensions={0} | all-to-all | bytes 262144 | tf_op jit(solution)/shard_map/all_to_all | solution.py:23
  81.2 0.6 reduce_sum.9
  (1 shorter events, 0.0 us)
Async XLA Ops:
  17.2 31.4 %all-to-all-start.1 = ((f32[128,5,1,128]{3,2,1,0:T(1,128)}), f32[128,5,1,128]{3,2,1,0:T(1,128)S(1)}, u32[]{:S(2)}, u32[]{:S(2)}) async-start(f32[128,5,1,128]{3,2,1,0:T(1,128)} %bitcast.5), calls=%async_computation.1 | async-start | bytes 655360 | tf_op jit(solution)/shard_map/all_to_all | solution.py:23
  48.6 7.7 %copy-start = (bf16[512,256]{1,0:T(8,128)(2,1)S(1)}, bf16[512,256]{1,0:T(8,128)(2,1)}, u32[]{:S(2)}) copy-start(bf16[512,256]{1,0:T(8,128)(2,1)} %param.11) | copy-start | bytes 786436
  51.0 17.5 %all-to-all-start.2 = ((bf16[64,8,128]{2,1,0:T(8,128)(2,1)}), bf16[64,8,128]{2,1,0:T(8,128)(2,1)S(1)}, u32[]{:S(2)}, u32[]{:S(2)}) async-start(bf16[64,8,128]{2,1,0:T(8,128)(2,1)} %bitcast.7), calls=%async_computation.2 | async-start | bytes 262144 | tf_op jit(solution)/shard_map/all_to_all | solution.py:23
  56.3 12.4 %collective-permute-start = (bf16[512,256]{1,0:T(8,128)(2,1)S(1)}, bf16[512,256]{1,0:T(8,128)(2,1)S(1)}, u32[]{:S(2)}, u32[]{:S(2)}) collective-permute-start(bf16[512,256]{1,0:T(8,128)(2,1)S(1)} %copy-done), channel_id=1, source_target_pairs={{0,3},{1,2},{2,1},{3,0},{4,7},{5,6},{6,5},{7,4},{8,11},{9,10},{10,... | collective-permute-start | bytes 786440 | tf_op jit(solution)/shard_map/ppermute | solution.py:260

commit v5 on v4

--- a/solution.py
+++ b/solution.py
@@ -12,6 +12,7 @@
 LANES = 128
 KEYS_STEP = 2048
 EARLY = 3072
+SCALE = 64.0
 WIDTH = ("z", "yh")
 GROUPS = ("yl", "core")
 ACROSS = ("xa", "xb")
@@ -78,14 +79,17 @@
     pieces = terms.shape[1] // LANES
     for piece in range(pieces):
         terms_ref[pl.ds(piece * rows, rows), :] = terms[:, piece * LANES : (piece + 1) * LANES]
+    held = out_ref.shape[0] // rows
     deep, near = 8, 4
     wide = rows // deep
     for place in range(wide):
         first = (place // near) * deep * near + place % near
         for piece in range(pieces):
-            out_ref[pl.ds(first * pieces + piece, deep, stride=near * pieces), :] = terms_ref[
+            out_ref[pl.ds(first * held + piece, deep, stride=near * held), :] = terms_ref[
                 pl.ds(piece * rows + place, deep, stride=wide), :
             ]
+    for piece in range(pieces, held):
+        out_ref[pl.ds(piece, rows, stride=held), :] = jnp.zeros((rows, LANES), jnp.float32)
 
 
 def attend(
@@ -117,9 +121,8 @@
     blocks = 4
     rows = received_ref.shape[0] // 32
     pieces = rows // blocks
-    heads = pieces - 1
-    sums = jnp.sum(received_ref[...].reshape(16, 2 * rows, LANES), axis=0)
-    mixed = sums[:rows] + sums[rows:]
+    heads = pieces - 2
+    mixed = jnp.sum(received_ref[...].reshape(32, rows, LANES), axis=0) * (1.0 / SCALE)
     mixed = mixed.astype(jnp.bfloat16).astype(jnp.float32)
     turned = mixed * turns_ref[0, :1] + pltpu.roll(mixed, LANES // 2, 1) * turns_ref[1, :1]
     turned = turned.astype(jnp.bfloat16).astype(jnp.float32)
@@ -130,7 +133,7 @@
     queries = queries_ref[...]
 
     def new(values, block):
-        return values[block * pieces + heads : (block + 1) * pieces]
+        return values[block * pieces + heads : block * pieces + heads + 1]
 
     scale = 1.0 / math.sqrt(LANES)
     row_group = lax.broadcasted_iota(jnp.int32, (4 * heads, 1), 0) // (2 * heads)
@@ -216,6 +219,7 @@
     hbm = pl.BlockSpec(memory_space=pltpu.HBM)
     anywhere = pl.BlockSpec(memory_space=pl.ANY)
     pieces = out_cols // head_dim
+    pairs = (pieces + 1) // 2
     copies, weights = pl.pallas_call(
         load,
         out_shape=(
@@ -233,12 +237,15 @@
     mine_t = exchange(copies, HEADS)
     sent = pl.pallas_call(
         project,
-        out_shape=jax.ShapeDtypeStruct((rows * pieces, head_dim), jnp.float32),
+        out_shape=jax.ShapeDtypeStruct((rows * 2 * pairs, head_dim), jnp.float32),
         in_specs=[vmem, vmem],
         out_specs=vmem,
-        scratch_shapes=[pltpu.VMEM((rows * pieces, head_dim), jnp.float32)],
+        scratch_shapes=[
+            pltpu.VMEM((rows * pieces, head_dim), jnp.float32),
+        ],
         compiler_params=pltpu.CompilerParams(vmem_limit_bytes=4 * 2**20),
     )(mine_t.reshape(-1, rows), weights)
+    halves = (sent * SCALE).astype(jnp.float16)
     span = k_cache.shape[1] * k_cache.shape[2]
     cache = jax.ShapeDtypeStruct((span, head_dim), k_cache.dtype)
     early_cache = jax.ShapeDtypeStruct((EARLY, head_dim), v_cache.dtype)
@@ -255,7 +262,7 @@
             flops=0, bytes_accessed=3 * span * head_dim, transcendentals=0
         ),
     )(lengths, sent, in_hbm(k_cache.reshape(span, head_dim)), old_values)
-    received = exchange(sent.reshape(rows, pieces, 1, head_dim), ("yh", "z") + ACROSS)
+    received = exchange(halves.reshape(rows, pairs, 2, head_dim), ("yh", "z") + ACROSS)
     w_late, _ = lax.optimization_barrier((w_out, sent))
     w_other = lax.ppermute(w_late, ACROSS, [(i, 3 - i) for i in range(4)])
     half = lax.axis_index("xa").reshape(1)
@@ -272,7 +279,7 @@
             pltpu.SemaphoreType.DMA((2,)),
         ],
         compiler_params=pltpu.CompilerParams(vmem_limit_bytes=8 * 2**20),
-    )(lengths, half, turns, received.reshape(-1, head_dim), keys, early, old_values)
+    )(lengths, half, turns, received.astype(jnp.float32).reshape(-1, head_dim), keys, early, old_values)
     near = WIDTH + ("xb",)
     mine = exchange(attended.reshape(rows // 2, heads // 2, head_dim), near)
     own_terms = jnp.einsum(

time: 82.2 us -> 79.5 us (0.967)
  waiting for transfers between devices: 23 us -> 20.3 us
    all_to_all x2, waiting for transfers between devices: 23 us -> 20.3 us  [exchange(): return lax.all_to_all(values, axes, split_axis=0, concat_axis=0, tiled=True)]
where the time goes in v5:
time: 79.5 us; the launch traced here: 79.1 us
  blocking collectives  27.2 us (34%)
  starting transfers between devices  23.2 us (29%)
  waiting for transfers between devices  20.3 us (26%)
  Pallas kernels  6.09 us (8%)
  other arithmetic  1.35 us (2%)
    all_to_all x2, blocking collectives, exchange(): return lax.all_to_all(values, axes, split_axis=0, concat_axis=0, tiled=True)  27.2 us
    all_to_all x2, waiting for transfers between devices, exchange(): return lax.all_to_all(values, axes, split_axis=0, concat_axis=0, tiled=True)  20.3 us
    all_to_all x2, starting transfers between devices, exchange(): return lax.all_to_all(values, axes, split_axis=0, concat_axis=0, tiled=True)  19.8 us
    ppermute x1, starting transfers between devices, shards(): w_other = lax.ppermute(w_late, ACROSS, [(i, 3 - i) for i in range(4)])  3.35 us
    pallas_call x1, Pallas kernels, shards(): pl.pallas_call(attend, out_shape=jax.ShapeDtypeStruct((32, heads, head_di...  2.43 us
    pallas_call x1, Pallas kernels, shards(): pl.pallas_call(fetch, out_shape=(cache, early_cache, jax.ShapeDtypeStruct...  1.79 us
  transfers between devices with their start and end apart: 3, of which 2 were waited for; matrix products, arithmetic and copies ran while one was open for 0% of the time, Pallas kernels for 2%

profile of v5, /device:TPU:1, one launch (start us, length us, event | category | flops | bytes accessed | tf_op | source)
XLA Modules:
  0.0 79.1 jit_solution(10720074786516281530)
XLA Ops:
  0.0 1.0 %shard_map.64 = (bf16[16,16,128]{2,1,0:T(8,128)(2,1)S(1)}, bf16[256,640]{1,0:T(8,128)(2,1)S(1)}) custom-call(bf16[16,128]{1,0:T(8,128)(2,1)} %bitcast.26, bf16[256,640]{1,0:T(8,128)(2,1)} %weights_ref.1), custom_call_target="tpu_custom_call" | custom-call | tf_op jit(solution)/shard_map/pallas_call | solution.py:223
  1.0 15.2 %all_to_all.20 = bf16[16,16,128]{2,1,0:T(8,128)(2,1)S(1)} all-to-all(bf16[16,16,128]{2,1,0:T(8,128)(2,1)S(1)} %get-tuple-element.11), channel_id=1, replica_groups=mesh['z'=8,'yh'=4,'yl'=2,'core'=2,'xa'=2,'xb'=2] {'yl','core','xa','xb'}, dimensions={0} | all-to-all | bytes 131072 | tf_op jit(solution)/shard_map/all_to_all | solution.py:24
  16.2 0.3 shard_map.65.after_ref
  16.5 0.7 multiply_convert_fusion
  17.2 14.7 %all-to-all-start.1 = ((f16[128,3,2,128]{3,2,1,0:T(2,128)(2,1)}), f16[128,3,2,128]{3,2,1,0:T(2,128)(2,1)S(1)}, u32[]{:S(2)}, u32[]{:S(2)}) async-start(f16[128,3,2,128]{3,2,1,0:T(2,128)(2,1)} %bitcast.5), calls=%async_computation.1 | async-start | bytes 393216 | tf_op jit(solution)/shard_map/all_to_all | solution.py:24
  32.6 1.8 %shard_map.66 = (bf16[8192,128]{1,0:T(8,128)(2,1)S(1)}, bf16[3072,128]{1,0:T(8,128)(2,1)S(1)}, f32[2,8,128]{2,1,0:T(8,128)S(1)}) custom-call(s32[1]{0:T(128)S(6)} %copy.13.length_ref, f32[768,128]{1,0:T(8,128)S(1)} %shard_map.65.after_ref, bf16[8192,128]{1,0:T(8,128)(2,1)} %bitcast.23, bf16[8192,128]{1,0:T(8,128)(2,1)} %bitcast.21), custom_call_target="tpu_custom_call" | custom-call | bytes 3145728 | tf_op jit(solution)/shard_map/pallas_call | solution.py:254
  34.4 11.5 %all-to-all-done.1 = f16[128,3,2,128]{3,2,1,0:T(2,128)(2,1)S(1)} async-done(((f16[128,3,2,128]{3,2,1,0:T(2,128)(2,1)}), f16[128,3,2,128]{3,2,1,0:T(2,128)(2,1)S(1)}, u32[]{:S(2)}, u32[]{:S(2)}) %all-to-all-start.1) | async-done | bytes 196640 | tf_op jit(solution)/shard_map/all_to_all | solution.py:24
  46.0 0.0 copy-start
  46.0 2.4 %shard_map.67 = bf16[32,16,128]{2,1,0:T(8,128)(2,1)} custom-call(s32[1]{0:T(128)S(6)} %copy.13.length_ref, s32[1]{0:T(128)} %bitcast.half_ref, f32[2,8,128]{2,1,0:T(8,128)S(1)} %get-tuple-element.13.turns_ref, f32[768,128]{1,0:T(8,128)S(1)} %convert.1.received_ref, bf16[8192,128]{1,0:T(8,128)(2,1)S(1)} %get-tuple-element.14.keys_ref, ...), custom_call_target="tpu_custom_call" | custom-call | tf_op jit(solution)/shard_map/pallas_call | solution.py:270
  48.4 5.1 %all-to-all-start.2 = ((bf16[64,8,128]{2,1,0:T(8,128)(2,1)}), bf16[64,8,128]{2,1,0:T(8,128)(2,1)S(1)}, u32[]{:S(2)}, u32[]{:S(2)}) async-start(bf16[64,8,128]{2,1,0:T(8,128)(2,1)} %bitcast.7), calls=%async_computation.2 | async-start | bytes 262144 | tf_op jit(solution)/shard_map/all_to_all | solution.py:24
  53.5 0.0 copy-done
  53.5 3.4 %collective-permute-start = (bf16[512,256]{1,0:T(8,128)(2,1)S(1)}, bf16[512,256]{1,0:T(8,128)(2,1)S(1)}, u32[]{:S(2)}, u32[]{:S(2)}) collective-permute-start(bf16[512,256]{1,0:T(8,128)(2,1)S(1)} %copy-done), channel_id=1, source_target_pairs={{0,3},{1,2},{2,1},{3,0},{4,7},{5,6},{6,5},{7,4},{8,11},{9,10},{10,... | collective-permute-start | bytes 786440 | tf_op jit(solution)/shard_map/ppermute | solution.py:267
  56.9 8.8 %all-to-all-done.2 = bf16[64,8,128]{2,1,0:T(8,128)(2,1)S(1)} async-done(((bf16[64,8,128]{2,1,0:T(8,128)(2,1)}), bf16[64,8,128]{2,1,0:T(8,128)(2,1)S(1)}, u32[]{:S(2)}, u32[]{:S(2)}) %all-to-all-start.2) | async-done | bytes 131104 | tf_op jit(solution)/shard_map/all_to_all | solution.py:24
  65.7 0.2 convolution_bitcast_fusion.first_ref
  65.8 0.0 collective-permute-done.weights_ref
  65.9 0.5 shard_map.68
  66.4 12.1 %all_to_all.21 = f32[16,16,128]{2,1,0:T(8,128)S(1)} all-to-all(f32[16,16,128]{2,1,0:T(8,128)S(1)} %bitcast.19), channel_id=1, replica_groups=mesh['z'=8,'yh'=4,'yl'=2,'core'=2,'xa'=2,'xb'=2] {'yl','core','xa','xb'}, dimensions={0} | all-to-all | bytes 262144 | tf_op jit(solution)/shard_map/all_to_all | solution.py:24
  78.5 0.6 reduce_sum.9
  (2 shorter events, 0.0 us)
Async XLA Ops:
  17.2 28.7 %all-to-all-start.1 = ((f16[128,3,2,128]{3,2,1,0:T(2,128)(2,1)}), f16[128,3,2,128]{3,2,1,0:T(2,128)(2,1)S(1)}, u32[]{:S(2)}, u32[]{:S(2)}) async-start(f16[128,3,2,128]{3,2,1,0:T(2,128)(2,1)} %bitcast.5), calls=%async_computation.1 | async-start | bytes 393216 | tf_op jit(solution)/shard_map/all_to_all | solution.py:24
  46.0 7.6 %copy-start = (bf16[512,256]{1,0:T(8,128)(2,1)S(1)}, bf16[512,256]{1,0:T(8,128)(2,1)}, u32[]{:S(2)}) copy-start(bf16[512,256]{1,0:T(8,128)(2,1)} %param.11) | copy-start | bytes 786436
  48.4 17.3 %all-to-all-start.2 = ((bf16[64,8,128]{2,1,0:T(8,128)(2,1)}), bf16[64,8,128]{2,1,0:T(8,128)(2,1)S(1)}, u32[]{:S(2)}, u32[]{:S(2)}) async-start(bf16[64,8,128]{2,1,0:T(8,128)(2,1)} %bitcast.7), calls=%async_computation.2 | async-start | bytes 262144 | tf_op jit(solution)/shard_map/all_to_all | solution.py:24
  53.5 12.3 %collective-permute-start = (bf16[512,256]{1,0:T(8,128)(2,1)S(1)}, bf16[512,256]{1,0:T(8,128)(2,1)S(1)}, u32[]{:S(2)}, u32[]{:S(2)}) collective-permute-start(bf16[512,256]{1,0:T(8,128)(2,1)S(1)} %copy-done), channel_id=1, source_target_pairs={{0,3},{1,2},{2,1},{3,0},{4,7},{5,6},{6,5},{7,4},{8,11},{9,10},{10,... | collective-permute-start | bytes 786440 | tf_op jit(solution)/shard_map/ppermute | solution.py:267

commit v6 on v4

--- a/solution.py
+++ b/solution.py
@@ -195,17 +195,16 @@
     sequence = lax.broadcasted_iota(jnp.int32, (count, 2 * count), 1)
     source = lax.broadcasted_iota(jnp.int32, (count, 2 * count), 0)
     place = source + 2 * (source // 2) + 2 * half_ref[0]
-    chosen = (sequence == place).astype(jnp.float32)
+    chosen = (sequence == place).astype(jnp.float32).astype(jnp.bfloat16)
     terms = first_ref[...] + jnp.dot(
         ours, weights_ref[...], preferred_element_type=jnp.float32
     )
     out_ref[...] = lax.dot_general(
-        terms,
+        terms.astype(jnp.bfloat16),
         chosen,
         (((0,), (0,)), ((), ())),
-        precision=lax.Precision.HIGHEST,
         preferred_element_type=jnp.float32,
-    )
+    ).astype(jnp.bfloat16)
 
 
 def shards(activations, w_qkv, k_cache, v_cache, lengths, w_out):
@@ -283,14 +282,14 @@
     )
     out_terms = pl.pallas_call(
         finish,
-        out_shape=jax.ShapeDtypeStruct((w_out.shape[1], rows), jnp.float32),
+        out_shape=jax.ShapeDtypeStruct((w_out.shape[1], rows), jnp.bfloat16),
         in_specs=[smem, vmem, vmem, vmem],
         out_specs=vmem,
         scratch_shapes=[pltpu.VMEM((rows * 4, head_dim), jnp.float32)],
         compiler_params=pltpu.CompilerParams(vmem_limit_bytes=4 * 2**20),
     )(half, own_terms, mine.reshape(-1, head_dim), w_other)
     out_parts = exchange(out_terms.reshape(16, -1, rows), HEADS)
-    return jnp.sum(out_parts, axis=0).astype(jnp.bfloat16).T
+    return jnp.sum(out_parts.astype(jnp.float32), axis=0).astype(jnp.bfloat16).T
 
 
 def solution(mesh):

time: 82.2 us -> 81.7 us (level)
  no operation moved by 1% of the time
where the time goes in v6:
time: 81.7 us; the launch traced here: 81.3 us
  blocking collectives  26.7 us (33%)
  starting transfers between devices  23.5 us (29%)
  waiting for transfers between devices  23 us (28%)
  Pallas kernels  6.66 us (8%)
    all_to_all x2, blocking collectives, exchange(): return lax.all_to_all(values, axes, split_axis=0, concat_axis=0, tiled=True)  26.7 us
    all_to_all x2, waiting for transfers between devices, exchange(): return lax.all_to_all(values, axes, split_axis=0, concat_axis=0, tiled=True)  23 us
    all_to_all x2, starting transfers between devices, exchange(): return lax.all_to_all(values, axes, split_axis=0, concat_axis=0, tiled=True)  20 us
    ppermute x1, starting transfers between devices, shards(): w_other = lax.ppermute(w_late, ACROSS, [(i, 3 - i) for i in range(4)])  3.45 us
    pallas_call x1, Pallas kernels, shards(): pl.pallas_call(attend, out_shape=jax.ShapeDtypeStruct((32, heads, head_di...  2.43 us
    pallas_call x1, Pallas kernels, shards(): pl.pallas_call(fetch, out_shape=(cache, early_cache, jax.ShapeDtypeStruct...  1.79 us
  transfers between devices with their start and end apart: 3, of which 2 were waited for; matrix products, arithmetic and copies ran while one was open for 0% of the time, Pallas kernels for 2%

profile of v6, /device:TPU:1, one launch (start us, length us, event | category | flops | bytes accessed | tf_op | source)
XLA Modules:
  0.0 81.3 jit_solution(7233003335068491379)
XLA Ops:
  0.0 1.0 %shard_map.64 = (bf16[16,16,128]{2,1,0:T(8,128)(2,1)S(1)}, bf16[256,640]{1,0:T(8,128)(2,1)S(1)}) custom-call(bf16[16,128]{1,0:T(8,128)(2,1)} %bitcast.23, bf16[256,640]{1,0:T(8,128)(2,1)} %weights_ref.1), custom_call_target="tpu_custom_call" | custom-call | tf_op jit(solution)/shard_map/pallas_call | solution.py:218
  1.0 15.2 %all_to_all.20 = bf16[16,16,128]{2,1,0:T(8,128)(2,1)S(1)} all-to-all(bf16[16,16,128]{2,1,0:T(8,128)(2,1)S(1)} %get-tuple-element.11), channel_id=1, replica_groups=mesh['z'=8,'yh'=4,'yl'=2,'core'=2,'xa'=2,'xb'=2] {'yl','core','xa','xb'}, dimensions={0} | all-to-all | bytes 131072 | tf_op jit(solution)/shard_map/all_to_all | solution.py:23
  16.2 1.0 %shard_map.65.after_ref = f32[640,128]{1,0:T(8,128)} custom-call(bf16[256,128]{1,0:T(8,128)(2,1)S(1)} %bitcast.18, bf16[256,640]{1,0:T(8,128)(2,1)S(1)} %get-tuple-element.12.weights_ref), custom_call_target="tpu_custom_call" | custom-call | tf_op jit(solution)/shard_map/pallas_call | solution.py:233
  17.2 14.7 %all-to-all-start.1 = ((f32[128,5,1,128]{3,2,1,0:T(1,128)}), f32[128,5,1,128]{3,2,1,0:T(1,128)S(1)}, u32[]{:S(2)}, u32[]{:S(2)}) async-start(f32[128,5,1,128]{3,2,1,0:T(1,128)} %bitcast.5), calls=%async_computation.1 | async-start | bytes 655360 | tf_op jit(solution)/shard_map/all_to_all | solution.py:23
  32.6 1.8 %shard_map.66 = (bf16[8192,128]{1,0:T(8,128)(2,1)S(1)}, bf16[3072,128]{1,0:T(8,128)(2,1)S(1)}, f32[2,8,128]{2,1,0:T(8,128)S(1)}) custom-call(s32[1]{0:T(128)S(6)} %copy.16.length_ref, f32[640,128]{1,0:T(8,128)} %shard_map.65.after_ref, bf16[8192,128]{1,0:T(8,128)(2,1)} %bitcast.21, bf16[8192,128]{1,0:T(8,128)(2,1)} %bitcast.19), custom_call_target="tpu_custom_call" | custom-call | bytes 3145728 | tf_op jit(solution)/shard_map/pallas_call | solution.py:246
  34.4 14.2 %all-to-all-done.1 = f32[128,5,1,128]{3,2,1,0:T(1,128)S(1)} async-done(((f32[128,5,1,128]{3,2,1,0:T(1,128)}), f32[128,5,1,128]{3,2,1,0:T(1,128)S(1)}, u32[]{:S(2)}, u32[]{:S(2)}) %all-to-all-start.1) | async-done | bytes 327712 | tf_op jit(solution)/shard_map/all_to_all | solution.py:23
  48.6 0.0 copy-start
  48.6 2.4 %shard_map.67 = bf16[32,16,128]{2,1,0:T(8,128)(2,1)} custom-call(s32[1]{0:T(128)S(6)} %copy.16.length_ref, s32[1]{0:T(128)} %bitcast.half_ref, f32[2,8,128]{2,1,0:T(8,128)S(1)} %get-tuple-element.13.turns_ref, f32[640,128]{1,0:T(8,128)S(1)} %bitcast.15, bf16[8192,128]{1,0:T(8,128)(2,1)S(1)} %get-tuple-element.14.keys_ref, ...), custom_call_target="tpu_custom_call" | custom-call | tf_op jit(solution)/shard_map/pallas_call | solution.py:262
  51.0 5.3 %all-to-all-start.2 = ((bf16[64,8,128]{2,1,0:T(8,128)(2,1)}), bf16[64,8,128]{2,1,0:T(8,128)(2,1)S(1)}, u32[]{:S(2)}, u32[]{:S(2)}) async-start(bf16[64,8,128]{2,1,0:T(8,128)(2,1)} %bitcast.7), calls=%async_computation.2 | async-start | bytes 262144 | tf_op jit(solution)/shard_map/all_to_all | solution.py:23
  56.3 0.0 copy-done
  56.3 3.4 %collective-permute-start = (bf16[512,256]{1,0:T(8,128)(2,1)S(1)}, bf16[512,256]{1,0:T(8,128)(2,1)S(1)}, u32[]{:S(2)}, u32[]{:S(2)}) collective-permute-start(bf16[512,256]{1,0:T(8,128)(2,1)S(1)} %copy-done), channel_id=1, source_target_pairs={{0,3},{1,2},{2,1},{3,0},{4,7},{5,6},{6,5},{7,4},{8,11},{9,10},{10,... | collective-permute-start | bytes 786440 | tf_op jit(solution)/shard_map/ppermute | solution.py:259
  59.8 8.8 %all-to-all-done.2 = bf16[64,8,128]{2,1,0:T(8,128)(2,1)S(1)} async-done(((bf16[64,8,128]{2,1,0:T(8,128)(2,1)}), bf16[64,8,128]{2,1,0:T(8,128)(2,1)S(1)}, u32[]{:S(2)}, u32[]{:S(2)}) %all-to-all-start.2) | async-done | bytes 131104 | tf_op jit(solution)/shard_map/all_to_all | solution.py:23
  68.6 0.2 convolution_bitcast_fusion.first_ref
  68.8 0.0 collective-permute-done.weights_ref
  68.8 0.4 shard_map.68
  69.2 11.5 %all_to_all.21 = bf16[16,16,128]{2,1,0:T(8,128)(2,1)S(1)} all-to-all(bf16[16,16,128]{2,1,0:T(8,128)(2,1)S(1)} %bitcast.17), channel_id=1, replica_groups=mesh['z'=8,'yh'=4,'yl'=2,'core'=2,'xa'=2,'xb'=2] {'yl','core','xa','xb'}, dimensions={0} | all-to-all | bytes 131072 | tf_op jit(solution)/shard_map/all_to_all | solution.py:23
  80.7 0.6 reduce_sum.12
  (1 shorter events, 0.0 us)
Async XLA Ops:
  17.2 31.4 %all-to-all-start.1 = ((f32[128,5,1,128]{3,2,1,0:T(1,128)}), f32[128,5,1,128]{3,2,1,0:T(1,128)S(1)}, u32[]{:S(2)}, u32[]{:S(2)}) async-start(f32[128,5,1,128]{3,2,1,0:T(1,128)} %bitcast.5), calls=%async_computation.1 | async-start | bytes 655360 | tf_op jit(solution)/shard_map/all_to_all | solution.py:23
  48.6 7.7 %copy-start = (bf16[512,256]{1,0:T(8,128)(2,1)S(1)}, bf16[512,256]{1,0:T(8,128)(2,1)}, u32[]{:S(2)}) copy-start(bf16[512,256]{1,0:T(8,128)(2,1)} %param.11) | copy-start | bytes 786436
  51.0 17.5 %all-to-all-start.2 = ((bf16[64,8,128]{2,1,0:T(8,128)(2,1)}), bf16[64,8,128]{2,1,0:T(8,128)(2,1)S(1)}, u32[]{:S(2)}, u32[]{:S(2)}) async-start(bf16[64,8,128]{2,1,0:T(8,128)(2,1)} %bitcast.7), calls=%async_computation.2 | async-start | bytes 262144 | tf_op jit(solution)/shard_map/all_to_all | solution.py:23
  56.3 12.4 %collective-permute-start = (bf16[512,256]{1,0:T(8,128)(2,1)S(1)}, bf16[512,256]{1,0:T(8,128)(2,1)S(1)}, u32[]{:S(2)}, u32[]{:S(2)}) collective-permute-start(bf16[512,256]{1,0:T(8,128)(2,1)S(1)} %copy-done), channel_id=1, source_target_pairs={{0,3},{1,2},{2,1},{3,0},{4,7},{5,6},{6,5},{7,4},{8,11},{9,10},{10,... | collective-permute-start | bytes 786440 | tf_op jit(solution)/shard_map/ppermute | solution.py:259
